TPU v7x, 32 devices: a whole 2x2x4 slice. The times are simulated.
32 devices in a mesh: groups: 2 (over x), wide: 16 (over z, y, core).
Axes of the slice: x: 2, y: 2, z: 4, core: 2. Of those that a mesh axis runs over, the one named last changes fastest.
Arguments:
- voltages: bfloat16 [512, 265216], P('wide', 'groups'), parts along dimension 1, may hold values from -6 to 6
- antenna_flags: int32 [1024], P(('groups', 'wide')), parts along dimension 0, may hold values 0 or 1
- baseline_pairs: int32 [2, 2048], replicated, may hold values from 0 to 511, as said below
Outputs:
- delay_power: float32 [512, 2048], P('groups', 'wide'), parts along dimension 0
There are 2 independent parts, one for each index of `groups`. A program takes and returns all parts, laid end to end along the dimension named above; an argument that names none is the same for every part. Nothing has to cross between parts.
Inputs may be any that keep to these rules, and one draw needn't show every extreme that they name: `baseline_pairs`: the two inputs of a baseline always differ; baseline 0 pairs input 0 with input 512 - 1.
All inputs are finite; a program needn't handle non-finite values. No bound on the sum of `antenna_flags` on one device may be relied on, other than what follows from the above.
Results may differ from a plain program's by a relative error of at most 0.0055.
Values may be sent and summed in bfloat16 or wider, within the bound.
A program may use at most 192 MiB of HBM per device.

v0:
```python
import functools
import math

import jax
import jax.numpy as jnp
import ml_dtypes
import numpy as np
from jax import lax
from jax.experimental import pallas as pl
from jax.experimental.pallas import tpu as pltpu
from jax.sharding import PartitionSpec as P

INPUT_COUNT = 512
CHANNEL_COUNT = 256
TAPS = 4
NT = 128
NFFT = 512


def prototype_table():
    count = TAPS * NFFT
    positions = jnp.arange(count, dtype=jnp.float32)
    start_shift = (positions - count / 2 + 0.5) / NFFT
    hamming = 0.54 - 0.46 * jnp.cos(2 * jnp.pi * positions / (count - 1))
    return (jnp.sinc(start_shift) * hamming).reshape(TAPS, NFFT)


def filter_bank(voltages, antenna_flags, first_input, count):
    framed = voltages.astype(jnp.float32).reshape(voltages.shape[0], -1, NFFT)
    prototype = prototype_table()
    filtered = jnp.zeros((voltages.shape[0], count, NFFT), jnp.float32)
    for tap_index in range(TAPS):
        filtered = (
            filtered
            + prototype[tap_index][None, None, :]
            * framed[:, first_input + tap_index : first_input + tap_index + count, :]
        )
    return filtered * antenna_flags.astype(jnp.float32)[:, None, None]


def transform_table():
    rows_int = jnp.arange(2 * CHANNEL_COUNT, dtype=jnp.int32)
    channel = rows_int // 2
    is_real = rows_int % 2 == 0
    sample = jnp.arange(NFFT, dtype=jnp.int32)
    phase = channel[:, None] * sample[None, :] % NFFT
    angle = 2 * jnp.pi * phase.astype(jnp.float32) / NFFT
    table = jnp.where(is_real[:, None], jnp.cos(angle), -jnp.sin(angle))
    return table / math.sqrt(NFFT)


def delay_table():
    chan_int = jnp.arange(CHANNEL_COUNT, dtype=jnp.int32)
    chan_float = chan_int.astype(jnp.float32)
    base = 2 * jnp.pi * chan_float / (CHANNEL_COUNT - 1)
    window = (
        0.35875
        - 0.48829 * jnp.cos(base)
        + 0.14128 * jnp.cos(2 * base)
        - 0.01168 * jnp.cos(3 * base)
    )
    phase = chan_int[:, None] * chan_int[None, :] % CHANNEL_COUNT
    angle = 2 * jnp.pi * phase.astype(jnp.float32) / CHANNEL_COUNT
    cosine = jnp.cos(angle) * window[None, :]
    sine = jnp.sin(angle) * window[None, :]
    upper = jnp.concatenate([cosine, sine], axis=1)
    lower = jnp.concatenate([-sine, cosine], axis=1)
    table = jnp.concatenate([upper, lower], axis=0) / jnp.sqrt(jnp.sum(window * window))
    return table.astype(jnp.bfloat16)


def correlate(received):
    values = received[0]
    swapped = jnp.stack([values[:, 1], -values[:, 0]], axis=1)
    stacked = jnp.stack([values, swapped], axis=0)
    return jnp.einsum("qcrit,crjt->iqcj", stacked, values, preferred_element_type=jnp.float32)


def per_device_general(voltages, antenna_flags, baseline_pairs):
    width = lax.axis_size("wide")
    local_inputs = voltages.shape[0]
    local_channels = CHANNEL_COUNT // width
    table = transform_table()
    scale = 1.0 / math.sqrt(2 * NT)
    correlation = jnp.zeros((INPUT_COUNT, 2, local_channels, INPUT_COUNT), jnp.float32)
    for batch_index in range(2):
        filtered = filter_bank(voltages, antenna_flags, batch_index * NT, NT)
        raw = jnp.einsum(
            "kn,itn->kit",
            table,
            filtered,
            precision=lax.Precision.HIGHEST,
            preferred_element_type=jnp.float32,
        )
        correlation = correlation + correlate(
            lax.all_to_all(
                raw.astype(jnp.bfloat16).reshape(width, local_channels, 2, local_inputs, NT),
                "wide",
                split_axis=0,
                concat_axis=3,
                tiled=True,
            )
        )
    baseline_count = baseline_pairs.shape[1]
    block_size = math.gcd(baseline_count, 1024)
    first_blocks = baseline_pairs[0].reshape(baseline_count // block_size, block_size)
    second_blocks = baseline_pairs[1].reshape(baseline_count // block_size, block_size)
    input_positions = jnp.arange(INPUT_COUNT, dtype=jnp.int32)

    def select_block(indices):
        first_block, second_block = indices
        rows_taken = jnp.take(correlation, first_block, axis=0)
        selector = (input_positions[None, :] == second_block[:, None]).astype(jnp.float32)
        return jnp.sum(rows_taken * selector[:, None, None, :], axis=3)

    selected = lax.map(select_block, (first_blocks, second_blocks))
    selected = selected.reshape(baseline_count, 2, local_channels)
    picked = (jnp.transpose(selected, (1, 2, 0)) * scale).astype(jnp.bfloat16)
    regrouped = lax.all_to_all(picked, "wide", split_axis=2, concat_axis=1, tiled=True)
    column_list = regrouped.reshape(2 * CHANNEL_COUNT, regrouped.shape[2])
    delays = jnp.dot(delay_table(), column_list, preferred_element_type=jnp.float32)
    return delays[:CHANNEL_COUNT] ** 2 + delays[CHANNEL_COUNT:] ** 2


LANES = 128
HALF = NFFT // 2
PIECES = 4
STEP = 4


def owned_channels(width):
    each = CHANNEL_COUNT // width // 2
    owner = np.arange(width)[:, None, None]
    parity = np.arange(2)[None, :, None]
    return 2 * (owner * each + np.arange(each)[None, None, :]) + parity


def split_transform_table(width):
    channel = owned_channels(width).transpose(1, 0, 2)[:, :, None, :, None]
    angle = 2 * np.pi * (channel * np.arange(HALF) % NFFT) / NFFT
    table = np.concatenate([np.cos(angle), -np.sin(angle)], axis=2) / math.sqrt(NFFT)
    table = table.reshape(2, -1, HALF).astype(np.float32)
    high = table.astype(ml_dtypes.bfloat16)
    low = (table - high.astype(np.float32)).astype(ml_dtypes.bfloat16)
    return np.concatenate([high, high, low], axis=2)


def ordered_delay_table(width):
    chan = np.arange(CHANNEL_COUNT)
    base = 2 * np.pi * chan / (CHANNEL_COUNT - 1)
    window = (
        0.35875 - 0.48829 * np.cos(base) + 0.14128 * np.cos(2 * base) - 0.01168 * np.cos(3 * base)
    )
    angle = 2 * np.pi * (chan[:, None] * chan[None, :] % CHANNEL_COUNT) / CHANNEL_COUNT
    cosine, sine = np.cos(angle) * window, np.sin(angle) * window
    table = np.block([[cosine, sine], [-sine, cosine]]) / np.sqrt(np.sum(window * window))
    channel = owned_channels(width)[:, :, None, :]
    order = channel + CHANNEL_COUNT * np.arange(2)[None, None, :, None]
    return table[:, order.reshape(-1)].astype(np.float32).astype(ml_dtypes.bfloat16)


def spectra_kernel(batch, volts, flags, proto, table, out, held, filt, sems):
    inputs = held.shape[0]
    piece = NT // PIECES
    copies = []
    for part in range(PIECES):
        frames = piece + (TAPS - 1 if part == PIECES - 1 else 0)
        copies.append(
            pltpu.make_async_copy(
                volts.at[:, pl.ds((batch * NT + part * piece) * NFFT, frames * NFFT)],
                held.at[:, pl.ds(part * piece * NFFT, frames * NFFT)],
                sems.at[part],
            )
        )
    for copy in copies:
        copy.start()
    copies[0].wait()
    for part in range(PIECES):
        if part + 1 < PIECES:
            copies[part + 1].wait()

        @pl.loop(part * piece // STEP, (part + 1) * piece // STEP)
        def _(step):
            first = step * STEP
            flag = flags[...]
            for block in range(2):
                sides = []
                for lane in (block * LANES, HALF + block * LANES):
                    frames = [
                        held[
                            :, pl.ds(pl.multiple_of((first + f) * NFFT + lane, LANES), LANES)
                        ].astype(jnp.float32)
                        for f in range(STEP + TAPS - 1)
                    ]
                    weights = [proto[tap : tap + 1, lane : lane + LANES] for tap in range(TAPS)]
                    sides.append(
                        [
                            sum(weights[tap] * frames[u + tap] for tap in range(TAPS)) * flag
                            for u in range(STEP)
                        ]
                    )
                for u in range(STEP):
                    rows = pl.ds(pl.multiple_of((first + u) * inputs, 8), inputs)
                    filt[block, rows, :] = sides[0][u] + sides[1][u]
                    filt[2 + block, rows, :] = sides[0][u] - sides[1][u]

    rows_each = out.shape[2] // 2

    @pl.loop(0, inputs, unroll=2)
    def _(a):
        for parity in range(2):
            x = jnp.concatenate(
                [filt[2 * parity + b, pl.ds(a, NT, stride=inputs), :] for b in range(2)], axis=1
            )
            high = x.astype(jnp.bfloat16)
            low = (x - high.astype(jnp.float32)).astype(jnp.bfloat16)
            result = lax.dot_general(
                table[parity],
                jnp.concatenate([high, low, high], axis=1),
                (((1,), (1,)), ((), ())),
                preferred_element_type=jnp.float32,
            )
            out[:, a, parity * rows_each : (parity + 1) * rows_each, :] = result.astype(
                jnp.bfloat16
            ).reshape(out.shape[0], rows_each, NT)


def make_spectra(batch, voltages, flags, proto, table, width):
    inputs = voltages.shape[0]
    rows = 2 * CHANNEL_COUNT // width
    vmem = pl.BlockSpec(memory_space=pltpu.VMEM)
    return pl.pallas_call(
        functools.partial(spectra_kernel, batch),
        out_shape=jax.ShapeDtypeStruct((width, inputs, rows, NT), jnp.bfloat16),
        in_specs=[pl.BlockSpec(memory_space=pl.ANY), vmem, vmem, vmem],
        out_specs=vmem,
        scratch_shapes=[
            pltpu.VMEM((inputs, (NT + TAPS - 1) * NFFT), jnp.bfloat16),
            pltpu.VMEM((4, NT * inputs, LANES), jnp.float32),
            pltpu.SemaphoreType.DMA((PIECES,)),
        ],
        compiler_params=pltpu.CompilerParams(vmem_limit_bytes=40 * 2**20),
        cost_estimate=pl.CostEstimate(
            flops=6 * 2 * CHANNEL_COUNT * HALF * NT * inputs,
            bytes_accessed=4 * NT * NFFT * inputs,
            transcendentals=0,
        ),
        name="spectra",
    )(voltages, flags, proto, table)


def baseline_kernel(last, pairs, values, *rest):
    before, out = rest if last else (None, rest[0])
    rows = values.shape[1]
    each = rows // 4
    lane = lax.broadcasted_iota(jnp.int32, (rows, LANES), 1)

    @pl.loop(0, out.shape[0])
    def _(block):
        def one(at, total):
            k = block * LANES + at
            a = values[pairs[0, k]].astype(jnp.float32)
            b = values[pairs[1, k]].astype(jnp.float32)
            products = []
            for start in (0, 2 * each):
                a_re, a_im = a[start : start + each], a[start + each : start + 2 * each]
                b_re, b_im = b[start : start + each], b[start + each : start + 2 * each]
                products.append(a_re * b_re + a_im * b_im)
                products.append(a_im * b_re - a_re * b_im)
            summed = jnp.sum(jnp.concatenate(products, axis=0), axis=1, keepdims=True)
            return jnp.where(lane == at, summed, total)

        total = lax.fori_loop(0, LANES, one, jnp.zeros((rows, LANES), jnp.float32), unroll=8)
        if last:
            total = (total + before[block]) * (1.0 / math.sqrt(2 * NT))
        out[block] = total.astype(out.dtype)


def correlate_baselines(pairs, values, before=None):
    last = before is not None
    count, rows = pairs.shape[1], values.shape[1]
    vmem = pl.BlockSpec(memory_space=pltpu.VMEM)
    return pl.pallas_call(
        functools.partial(baseline_kernel, last),
        out_shape=jax.ShapeDtypeStruct(
            (count // LANES, rows, LANES), jnp.bfloat16 if last else jnp.float32
        ),
        in_specs=[pl.BlockSpec(memory_space=pltpu.SMEM), vmem] + [vmem] * last,
        out_specs=vmem,
        compiler_params=pltpu.CompilerParams(vmem_limit_bytes=32 * 2**20),
        cost_estimate=pl.CostEstimate(
            flops=4 * count * rows * NT,
            bytes_accessed=2 * values.size,
            transcendentals=0,
        ),
        name="baselines",
    )(pairs, values, *([before] if last else []))


def per_device(voltages, antenna_flags, baseline_pairs):
    width = lax.axis_size("wide")
    inputs = voltages.shape[0]
    count = baseline_pairs.shape[1]
    rows = 2 * CHANNEL_COUNT // width
    if rows % 32 or inputs % 8 or count // width != LANES:
        return per_device_general(voltages, antenna_flags, baseline_pairs)
    flags = jnp.broadcast_to(antenna_flags.astype(jnp.float32)[:, None], (inputs, LANES))
    proto = prototype_table()
    table = jnp.asarray(split_transform_table(width))
    total = None
    for batch in range(2):
        sent = make_spectra(batch, voltages, flags, proto, table, width)
        received = lax.all_to_all(sent, "wide", split_axis=0, concat_axis=0, tiled=True)
        total = correlate_baselines(
            baseline_pairs, received.reshape(width * inputs, rows, NT), total
        )
    columns = lax.all_to_all(total, "wide", split_axis=0, concat_axis=0, tiled=True)
    delays = jnp.dot(
        jnp.asarray(ordered_delay_table(width)),
        columns.reshape(2 * CHANNEL_COUNT, LANES),
        preferred_element_type=jnp.float32,
    )
    return delays[:CHANNEL_COUNT] ** 2 + delays[CHANNEL_COUNT:] ** 2


def solution(mesh):
    placed = (P("wide", "groups"), P(("groups", "wide")), P())
    return jax.shard_map(
        per_device, mesh=mesh, in_specs=placed, out_specs=P("groups", "wide"), check_vma=False
    )
```

profile of v0, /device:TPU:0, one launch (start us, length us, event | category | flops | bytes accessed | tf_op | source)
XLA Modules:
  0.0 269.0 jit_solution(7157488073537598476)
XLA Ops:
  0.0 0.1 fusion.6.proto
  0.1 0.7 convert_element_type.8
  0.8 0.1 broadcast_in_dim.11.flags
  0.8 0.0 copy-start
  0.8 3.4 %copy-done = bf16[32,132608]{1,0:T(8,128)(2,1)S(1)} copy-done((bf16[32,132608]{1,0:T(8,128)(2,1)S(1)}, bf16[32,132608]{1,0:T(8,128)(2,1)}, u32[]{:S(2)}) %copy-start) | copy-done | bytes 8486936
  4.2 0.0 copy-start.4
  4.2 1.1 copy-done.4
  5.4 19.5 %spectra.3 = bf16[16,32,32,128]{3,2,1,0:T(8,128)(2,1)S(1)} custom-call(bf16[32,132608]{1,0:T(8,128)(2,1)S(1)} %copy-done, f32[32,128]{1,0:T(8,128)S(1)} %broadcast_in_dim.11.flags, f32[4,512]{1,0:T(4,128)S(1)} %fusion.6.proto, bf16[2,256,768]{2,1,0:T(8,128)(2,1)S(1)} %copy-done.4), custom_call_target="tpu_custom_call" | custom-call | flops 3221225472 | bytes 8388608 | tf_op jit(solution)/shard_map/spectra/pallas_call | solution.py:232
  24.9 0.0 copy-start.3
  24.9 2.0 copy-done.3
  26.8 0.0 copy-start.5
  26.8 7.5 %all-to-all-start.1 = ((bf16[16,32,32,128]{3,2,1,0:T(8,128)(2,1)}), bf16[16,32,32,128]{3,2,1,0:T(8,128)(2,1)}, u32[]{:S(2)}, u32[]{:S(2)}) async-start(bf16[16,32,32,128]{3,2,1,0:T(8,128)(2,1)} %copy-done.3), calls=%async_computation.1 | async-start | bytes 8388608 | tf_op jit(solution)/shard_map/all_to_all | solution.py:313
  34.4 0.0 copy-done.5
  34.4 0.0 copy-start.1
  34.4 3.4 %copy-done.1 = bf16[32,132608]{1,0:T(8,128)(2,1)S(1)} copy-done((bf16[32,132608]{1,0:T(8,128)(2,1)S(1)}, bf16[32,132608]{1,0:T(8,128)(2,1)}, u32[]{:S(2)}) %copy-start.1) | copy-done | bytes 8486936
  37.8 19.5 %spectra.2 = bf16[16,32,32,128]{3,2,1,0:T(8,128)(2,1)S(1)} custom-call(bf16[32,132608]{1,0:T(8,128)(2,1)S(1)} %copy-done.1, f32[32,128]{1,0:T(8,128)S(1)} %broadcast_in_dim.11.flags, f32[4,512]{1,0:T(4,128)S(1)} %fusion.6.proto, bf16[2,256,768]{2,1,0:T(8,128)(2,1)S(1)} %copy-done.5), custom_call_target="tpu_custom_call" | custom-call | flops 3221225472 | bytes 8388608 | tf_op jit(solution)/shard_map/spectra/pallas_call | solution.py:232
  57.3 0.0 copy-start.2
  57.3 2.0 copy-done.2
  59.3 0.0 copy-start.6
  59.3 52.8 %all-to-all-done.1 = bf16[16,32,32,128]{3,2,1,0:T(8,128)(2,1)} async-done(((bf16[16,32,32,128]{3,2,1,0:T(8,128)(2,1)}), bf16[16,32,32,128]{3,2,1,0:T(8,128)(2,1)}, u32[]{:S(2)}, u32[]{:S(2)}) %all-to-all-start.1) | async-done | bytes 4194336 | tf_op jit(solution)/shard_map/all_to_all | solution.py:313
  112.0 19.7 %all-to-all-start = ((bf16[16,32,32,128]{3,2,1,0:T(8,128)(2,1)}), bf16[16,32,32,128]{3,2,1,0:T(8,128)(2,1)}, u32[]{:S(2)}, u32[]{:S(2)}) async-start(bf16[16,32,32,128]{3,2,1,0:T(8,128)(2,1)} %copy-done.2), calls=%async_computation | async-start | bytes 8388608 | tf_op jit(solution)/shard_map/all_to_all | solution.py:313
  131.7 0.0 copy-done.6
  131.8 0.0 copy-start.7
  131.8 31.3 %baselines.2.rest_0_ = f32[16,32,128]{2,1,0:T(8,128)S(1)} custom-call(s32[2,2048]{1,0:T(2,128)S(1)} %copy-done.6, bf16[512,32,128]{2,1,0:T(8,128)(2,1)} %bitcast.1.values), custom_call_target="tpu_custom_call" | custom-call | flops 33554432 | bytes 4194304 | tf_op jit(solution)/shard_map/baselines/pallas_call | solution.py:283
  163.1 46.4 %all-to-all-done = bf16[16,32,32,128]{3,2,1,0:T(8,128)(2,1)} async-done(((bf16[16,32,32,128]{3,2,1,0:T(8,128)(2,1)}), bf16[16,32,32,128]{3,2,1,0:T(8,128)(2,1)}, u32[]{:S(2)}, u32[]{:S(2)}) %all-to-all-start) | async-done | bytes 4194336 | tf_op jit(solution)/shard_map/all_to_all | solution.py:313
  209.4 31.2 %baselines.3 = bf16[16,32,128]{2,1,0:T(8,128)(2,1)S(1)} custom-call(s32[2,2048]{1,0:T(2,128)S(1)} %copy-done.6, bf16[512,32,128]{2,1,0:T(8,128)(2,1)} %bitcast.values, f32[16,32,128]{2,1,0:T(8,128)S(1)} %baselines.2.rest_0_), custom_call_target="tpu_custom_call" | custom-call | flops 33554432 | bytes 4194304 | tf_op jit(solution)/shard_map/baselines/pallas_call | solution.py:283
  240.7 27.4 %all_to_all.15 = bf16[16,32,128]{2,1,0:T(8,128)(2,1)S(1)} all-to-all(bf16[16,32,128]{2,1,0:T(8,128)(2,1)S(1)} %baselines.3), channel_id=1, replica_groups=mesh['groups'=2,'wide'=16] {'wide'}, dimensions={0} | all-to-all | bytes 262144 | tf_op jit(solution)/shard_map/all_to_all | solution.py:317
  268.0 0.0 copy-done.7
  268.0 0.3 fusion.12
  268.3 0.7 fusion
Async XLA Ops:
  0.8 3.4 %copy-start = (bf16[32,132608]{1,0:T(8,128)(2,1)S(1)}, bf16[32,132608]{1,0:T(8,128)(2,1)}, u32[]{:S(2)}) copy-start(bf16[32,132608]{1,0:T(8,128)(2,1)} %volts.3) | copy-start | bytes 25460740
  4.2 1.1 copy-start.4
  24.9 2.0 copy-start.3
  26.8 7.5 %copy-start.5 = (bf16[2,256,768]{2,1,0:T(8,128)(2,1)S(1)}, bf16[2,256,768]{2,1,0:T(8,128)(2,1)}, u32[]{:S(2)}) copy-start(bf16[2,256,768]{2,1,0:T(8,128)(2,1)} %constant.63.clone.table) | copy-start | bytes 2359300
  26.8 85.2 %all-to-all-start.1 = ((bf16[16,32,32,128]{3,2,1,0:T(8,128)(2,1)}), bf16[16,32,32,128]{3,2,1,0:T(8,128)(2,1)}, u32[]{:S(2)}, u32[]{:S(2)}) async-start(bf16[16,32,32,128]{3,2,1,0:T(8,128)(2,1)} %copy-done.3), calls=%async_computation.1 | async-start | bytes 8388608 | tf_op jit(solution)/shard_map/all_to_all | solution.py:313
  34.4 3.4 %copy-start.1 = (bf16[32,132608]{1,0:T(8,128)(2,1)S(1)}, bf16[32,132608]{1,0:T(8,128)(2,1)}, u32[]{:S(2)}) copy-start(bf16[32,132608]{1,0:T(8,128)(2,1)} %volts.3) | copy-start | bytes 25460740
  57.3 2.0 copy-start.2
  59.3 72.5 %copy-start.6 = (s32[2,2048]{1,0:T(2,128)S(1)}, s32[2,2048]{1,0:T(2,128)}, u32[]{:S(2)}) copy-start(s32[2,2048]{1,0:T(2,128)} %pairs.3) | copy-start | bytes 49156
  112.0 97.4 %all-to-all-start = ((bf16[16,32,32,128]{3,2,1,0:T(8,128)(2,1)}), bf16[16,32,32,128]{3,2,1,0:T(8,128)(2,1)}, u32[]{:S(2)}, u32[]{:S(2)}) async-start(bf16[16,32,32,128]{3,2,1,0:T(8,128)(2,1)} %copy-done.2), calls=%async_computation | async-start | bytes 8388608 | tf_op jit(solution)/shard_map/all_to_all | solution.py:313
  131.8 136.3 %copy-start.7 = (bf16[512,512]{1,0:T(8,128)(2,1)S(1)}, bf16[512,512]{1,0:T(8,128)(2,1)}, u32[]{:S(2)}) copy-start(bf16[512,512]{1,0:T(8,128)(2,1)} %constant.64.clone) | copy-start | bytes 1572868
where the time goes:
time: 269 us
  Pallas kernels  102 us (38%)
  waiting for transfers between devices  99.1 us (37%)
  blocking collectives  27.4 us (10%)
  starting transfers between devices  27.2 us (10%)
  local copies, waits for them, and re-layouts  11.9 us (4%)
    all_to_all x2, waiting for transfers between devices, per_device(): lax.all_to_all(sent, 'wide', split_axis=0, concat_axis=0, tiled=True)  99.1 us
    pallas_call x2, Pallas kernels, correlate_baselines(): pl.pallas_call(functools.partial(baseline_kernel, last), out_shape=jax.Sh...  62.5 us
    pallas_call x2, Pallas kernels, make_spectra(): pl.pallas_call(functools.partial(spectra_kernel, batch), out_shape=jax.Sh...  39 us
    all_to_all x1, blocking collectives, per_device(): lax.all_to_all(total, 'wide', split_axis=0, concat_axis=0, tiled=True)  27.4 us
    all_to_all x2, starting transfers between devices, per_device(): lax.all_to_all(sent, 'wide', split_axis=0, concat_axis=0, tiled=True)  27.2 us
    unnamed x16, local copies, waits for them, and re-layouts  11.9 us
  transfers between devices with their start and end apart: 2, of which 2 were waited for; matrix products, arithmetic and copies ran while one was open for 0% of the time, Pallas kernels for 19%

commit v1 on v0

--- a/solution.py
+++ b/solution.py
@@ -126,6 +126,7 @@
 HALF = NFFT // 2
 PIECES = 4
 STEP = 4
+TOGETHER = 8
 
 
 def owned_channels(width):
@@ -159,8 +160,9 @@
     return table[:, order.reshape(-1)].astype(np.float32).astype(ml_dtypes.bfloat16)
 
 
-def spectra_kernel(batch, volts, flags, proto, table, out, held, filt, sems):
+def spectra_kernel(batch, volts, flags, proto, table_far, out, held, filt, table, sems):
     inputs = held.shape[0]
+    table_copy = pltpu.make_async_copy(table_far, table, sems.at[PIECES])
     piece = NT // PIECES
     copies = []
     for part in range(PIECES):
@@ -174,6 +176,7 @@
         )
     for copy in copies:
         copy.start()
+    table_copy.start()
     copies[0].wait()
     for part in range(PIECES):
         if part + 1 < PIECES:
@@ -204,6 +207,7 @@
                     filt[block, rows, :] = sides[0][u] + sides[1][u]
                     filt[2 + block, rows, :] = sides[0][u] - sides[1][u]
 
+    table_copy.wait()
     rows_each = out.shape[2] // 2
 
     @pl.loop(0, inputs, unroll=2)
@@ -229,15 +233,17 @@
     inputs = voltages.shape[0]
     rows = 2 * CHANNEL_COUNT // width
     vmem = pl.BlockSpec(memory_space=pltpu.VMEM)
+    anywhere = pl.BlockSpec(memory_space=pl.ANY)
     return pl.pallas_call(
         functools.partial(spectra_kernel, batch),
         out_shape=jax.ShapeDtypeStruct((width, inputs, rows, NT), jnp.bfloat16),
-        in_specs=[pl.BlockSpec(memory_space=pl.ANY), vmem, vmem, vmem],
+        in_specs=[anywhere, vmem, vmem, anywhere],
         out_specs=vmem,
         scratch_shapes=[
             pltpu.VMEM((inputs, (NT + TAPS - 1) * NFFT), jnp.bfloat16),
             pltpu.VMEM((4, NT * inputs, LANES), jnp.float32),
-            pltpu.SemaphoreType.DMA((PIECES,)),
+            pltpu.VMEM(table.shape, table.dtype),
+            pltpu.SemaphoreType.DMA((PIECES + 1,)),
         ],
         compiler_params=pltpu.CompilerParams(vmem_limit_bytes=40 * 2**20),
         cost_estimate=pl.CostEstimate(
@@ -249,28 +255,49 @@
     )(voltages, flags, proto, table)
 
 
+def fold(parts, shift, lane):
+    first = lane & shift == 0
+    return [
+        jnp.where(first, u, v) + pltpu.roll(jnp.where(first, v, u), shift, 1)
+        for u, v in zip(parts[::2], parts[1::2])
+    ]
+
+
 def baseline_kernel(last, pairs, values, *rest):
-    before, out = rest if last else (None, rest[0])
+    before, out, partial = rest if last else (None, *rest)
     rows = values.shape[1]
     each = rows // 4
     lane = lax.broadcasted_iota(jnp.int32, (rows, LANES), 1)
 
+    def products(k):
+        a = values[pairs[0, k]].astype(jnp.float32)
+        b = values[pairs[1, k]].astype(jnp.float32)
+        terms = []
+        for start in (0, 2 * each):
+            a_re, a_im = a[start : start + each], a[start + each : start + 2 * each]
+            b_re, b_im = b[start : start + each], b[start + each : start + 2 * each]
+            terms.append(a_re * b_re + a_im * b_im)
+            terms.append(a_im * b_re - a_re * b_im)
+        return jnp.concatenate(terms, axis=0)
+
     @pl.loop(0, out.shape[0])
     def _(block):
-        def one(at, total):
-            k = block * LANES + at
-            a = values[pairs[0, k]].astype(jnp.float32)
-            b = values[pairs[1, k]].astype(jnp.float32)
-            products = []
-            for start in (0, 2 * each):
-                a_re, a_im = a[start : start + each], a[start + each : start + 2 * each]
-                b_re, b_im = b[start : start + each], b[start + each : start + 2 * each]
-                products.append(a_re * b_re + a_im * b_im)
-                products.append(a_im * b_re - a_re * b_im)
-            summed = jnp.sum(jnp.concatenate(products, axis=0), axis=1, keepdims=True)
-            return jnp.where(lane == at, summed, total)
-
-        total = lax.fori_loop(0, LANES, one, jnp.zeros((rows, LANES), jnp.float32), unroll=8)
+        @pl.loop(0, LANES // TOGETHER, unroll=2)
+        def _(group):
+            start = block * LANES + group * TOGETHER
+            parts = [products(start + at) for at in range(TOGETHER)]
+            shift = 1
+            while len(parts) > 1:
+                parts = fold(parts, shift, lane)
+                shift *= 2
+            partial[group] = parts[0]
+
+        parts = [partial[group] for group in range(LANES // TOGETHER)]
+        shift = TOGETHER
+        while len(parts) > 1:
+            parts = fold(parts, shift, lane)
+            shift *= 2
+        total = parts[0]
         if last:
             total = (total + before[block]) * (1.0 / math.sqrt(2 * NT))
         out[block] = total.astype(out.dtype)
@@ -287,6 +314,7 @@
         ),
         in_specs=[pl.BlockSpec(memory_space=pltpu.SMEM), vmem] + [vmem] * last,
         out_specs=vmem,
+        scratch_shapes=[pltpu.VMEM((LANES // TOGETHER, rows, LANES), jnp.float32)],
         compiler_params=pltpu.CompilerParams(vmem_limit_bytes=32 * 2**20),
         cost_estimate=pl.CostEstimate(
             flops=4 * count * rows * NT,
@@ -295,6 +323,57 @@
         ),
         name="baselines",
     )(pairs, values, *([before] if last else []))
+
+
+def exchange_kernel(width, sent, out, send_sems, recv_sems, own_sem):
+    me = lax.axis_index("wide")
+    barrier = pltpu.get_barrier_semaphore()
+    for shift in range(1, width):
+        pl.semaphore_signal(
+            barrier,
+            inc=1,
+            device_id={"wide": lax.rem(me + shift, width)},
+            device_id_type=pl.DeviceIdType.MESH,
+        )
+    own = pltpu.make_async_copy(sent.at[me], out.at[me], own_sem)
+    own.start()
+    pl.semaphore_wait(barrier, width - 1)
+    copies = []
+    for shift in range(1, width):
+        other = lax.rem(me + shift, width)
+        copies.append(
+            pltpu.make_async_remote_copy(
+                src_ref=sent.at[other],
+                dst_ref=out.at[me],
+                send_sem=send_sems.at[shift],
+                recv_sem=recv_sems.at[shift],
+                device_id={"wide": other},
+                device_id_type=pl.DeviceIdType.MESH,
+            )
+        )
+        copies[-1].start()
+    own.wait()
+    for copy in copies:
+        copy.wait_recv()
+    for copy in copies:
+        copy.wait_send()
+
+
+def exchange(sent, width):
+    vmem = pl.BlockSpec(memory_space=pltpu.VMEM)
+    return pl.pallas_call(
+        functools.partial(exchange_kernel, width),
+        out_shape=jax.ShapeDtypeStruct(sent.shape, sent.dtype),
+        in_specs=[vmem],
+        out_specs=vmem,
+        scratch_shapes=[
+            pltpu.SemaphoreType.DMA((width,)),
+            pltpu.SemaphoreType.DMA((width,)),
+            pltpu.SemaphoreType.DMA,
+        ],
+        compiler_params=pltpu.CompilerParams(collective_id=0, has_side_effects=True),
+        name="exchange",
+    )(sent)
 
 
 def per_device(voltages, antenna_flags, baseline_pairs):
@@ -314,7 +393,7 @@
         total = correlate_baselines(
             baseline_pairs, received.reshape(width * inputs, rows, NT), total
         )
-    columns = lax.all_to_all(total, "wide", split_axis=0, concat_axis=0, tiled=True)
+    columns = exchange(total, width)
     delays = jnp.dot(
         jnp.asarray(ordered_delay_table(width)),
         columns.reshape(2 * CHANNEL_COUNT, LANES),

time: 269 us -> 278 us (1.033)
  Pallas kernels: 102 us -> 145 us
  blocking collectives: 27.4 us -> 0 us
  waiting for transfers between devices: 99.1 us -> 89.1 us
    all_to_all x1 -> x0, blocking collectives: 27.4 us -> none  [per_device(): lax.all_to_all(total, 'wide', split_axis=0, concat_axis=0, tiled=True)]
    pallas_call x0 -> x1, Pallas kernels: none -> 23.8 us  [exchange(): pl.pallas_call(functools.partial(exchange_kernel, width), out_shape=jax.S...]
    pallas_call x2, Pallas kernels: 62.5 us -> 82.4 us  [correlate_baselines(): pl.pallas_call(functools.partial(baseline_kernel, last), out_shape=jax.Sh...]
    all_to_all x2, waiting for transfers between devices: 99.1 us -> 89.1 us  [per_device(): lax.all_to_all(sent, 'wide', split_axis=0, concat_axis=0, tiled=True)]
    unnamed x16 -> x18, local copies, waits for them, and re-layouts: 11.9 us -> 12.5 us
  transfers between devices with their start and end apart: 2 -> 2, of which waited for: 2 -> 2; matrix products, arithmetic and copies ran while one was open for 0% -> 0% of each run, Pallas kernels for 19% -> 22%
where the time goes in v1:
time: 278 us; the launch traced here: 277 us
  Pallas kernels  145 us (52%)
  waiting for transfers between devices  89.1 us (32%)
  starting transfers between devices  27.3 us (10%)
  local copies, waits for them, and re-layouts  12.6 us (5%)
    all_to_all x2, waiting for transfers between devices, per_device(): lax.all_to_all(sent, 'wide', split_axis=0, concat_axis=0, tiled=True)  89.1 us
    pallas_call x2, Pallas kernels, correlate_baselines(): pl.pallas_call(functools.partial(baseline_kernel, last), out_shape=jax.Sh...  82.4 us
    pallas_call x2, Pallas kernels, make_spectra(): pl.pallas_call(functools.partial(spectra_kernel, batch), out_shape=jax.Sh...  39.2 us
    all_to_all x2, starting transfers between devices, per_device(): lax.all_to_all(sent, 'wide', split_axis=0, concat_axis=0, tiled=True)  27.3 us
    pallas_call x1, Pallas kernels, exchange(): pl.pallas_call(functools.partial(exchange_kernel, width), out_shape=jax.S...  23.8 us
    unnamed x18, local copies, waits for them, and re-layouts  12.5 us
  transfers between devices with their start and end apart: 2, of which 2 were waited for; matrix products, arithmetic and copies ran while one was open for 0% of the time, Pallas kernels for 22%

profile of v1, /device:TPU:0, one launch (start us, length us, event | category | flops | bytes accessed | tf_op | source)
XLA Modules:
  0.0 277.1 jit_solution(3879879145310814320)
XLA Ops:
  0.0 0.1 fusion.6.proto
  0.1 0.7 convert_element_type.8
  0.8 0.1 broadcast_in_dim.11.flags
  0.8 0.0 copy-start
  0.8 3.4 %copy-done = bf16[32,132608]{1,0:T(8,128)(2,1)S(1)} copy-done((bf16[32,132608]{1,0:T(8,128)(2,1)S(1)}, bf16[32,132608]{1,0:T(8,128)(2,1)}, u32[]{:S(2)}) %copy-start) | copy-done | bytes 8486936
  4.2 0.0 copy-start.4
  4.2 1.1 copy-done.4
  5.4 19.6 %spectra.3 = bf16[16,32,32,128]{3,2,1,0:T(8,128)(2,1)S(1)} custom-call(bf16[32,132608]{1,0:T(8,128)(2,1)S(1)} %copy-done, f32[32,128]{1,0:T(8,128)S(1)} %broadcast_in_dim.11.flags, f32[4,512]{1,0:T(4,128)S(1)} %fusion.6.proto, bf16[2,256,768]{2,1,0:T(8,128)(2,1)S(1)} %copy-done.4), custom_call_target="tpu_custom_call" | custom-call | flops 3221225472 | bytes 8388608 | tf_op jit(solution)/shard_map/spectra/pallas_call | solution.py:237
  25.0 0.0 copy-start.3
  25.0 1.9 copy-done.3
  26.9 0.0 copy-start.5
  26.9 7.6 %all-to-all-start.1 = ((bf16[16,32,32,128]{3,2,1,0:T(8,128)(2,1)}), bf16[16,32,32,128]{3,2,1,0:T(8,128)(2,1)}, u32[]{:S(2)}, u32[]{:S(2)}) async-start(bf16[16,32,32,128]{3,2,1,0:T(8,128)(2,1)} %copy-done.3), calls=%async_computation.1 | async-start | bytes 8388608 | tf_op jit(solution)/shard_map/all_to_all | solution.py:392
  34.5 0.0 copy-done.5
  34.5 0.0 copy-start.1
  34.5 3.4 %copy-done.1 = bf16[32,132608]{1,0:T(8,128)(2,1)S(1)} copy-done((bf16[32,132608]{1,0:T(8,128)(2,1)S(1)}, bf16[32,132608]{1,0:T(8,128)(2,1)}, u32[]{:S(2)}) %copy-start.1) | copy-done | bytes 8486936
  37.9 19.6 %spectra.2 = bf16[16,32,32,128]{3,2,1,0:T(8,128)(2,1)S(1)} custom-call(bf16[32,132608]{1,0:T(8,128)(2,1)S(1)} %copy-done.1, f32[32,128]{1,0:T(8,128)S(1)} %broadcast_in_dim.11.flags, f32[4,512]{1,0:T(4,128)S(1)} %fusion.6.proto, bf16[2,256,768]{2,1,0:T(8,128)(2,1)S(1)} %copy-done.5), custom_call_target="tpu_custom_call" | custom-call | flops 3221225472 | bytes 8388608 | tf_op jit(solution)/shard_map/spectra/pallas_call | solution.py:237
  57.5 0.0 copy-start.2
  57.5 2.0 copy-done.2
  59.5 0.0 copy-start.7
  59.5 52.7 %all-to-all-done.1 = bf16[16,32,32,128]{3,2,1,0:T(8,128)(2,1)} async-done(((bf16[16,32,32,128]{3,2,1,0:T(8,128)(2,1)}), bf16[16,32,32,128]{3,2,1,0:T(8,128)(2,1)}, u32[]{:S(2)}, u32[]{:S(2)}) %all-to-all-start.1) | async-done | bytes 4194336 | tf_op jit(solution)/shard_map/all_to_all | solution.py:392
  112.2 19.7 %all-to-all-start = ((bf16[16,32,32,128]{3,2,1,0:T(8,128)(2,1)}), bf16[16,32,32,128]{3,2,1,0:T(8,128)(2,1)}, u32[]{:S(2)}, u32[]{:S(2)}) async-start(bf16[16,32,32,128]{3,2,1,0:T(8,128)(2,1)} %copy-done.2), calls=%async_computation | async-start | bytes 8388608 | tf_op jit(solution)/shard_map/all_to_all | solution.py:392
  131.9 0.0 copy-done.7
  131.9 0.0 copy-start.8
  131.9 41.2 %baselines.2.rest_0_ = f32[16,32,128]{2,1,0:T(8,128)S(1)} custom-call(s32[2,2048]{1,0:T(2,128)S(1)} %copy-done.7, bf16[512,32,128]{2,1,0:T(8,128)(2,1)} %bitcast.1.values), custom_call_target="tpu_custom_call" | custom-call | flops 33554432 | bytes 4194304 | tf_op jit(solution)/shard_map/baselines/pallas_call | solution.py:310
  173.1 36.4 %all-to-all-done = bf16[16,32,32,128]{3,2,1,0:T(8,128)(2,1)} async-done(((bf16[16,32,32,128]{3,2,1,0:T(8,128)(2,1)}), bf16[16,32,32,128]{3,2,1,0:T(8,128)(2,1)}, u32[]{:S(2)}, u32[]{:S(2)}) %all-to-all-start) | async-done | bytes 4194336 | tf_op jit(solution)/shard_map/all_to_all | solution.py:392
  209.6 41.2 %baselines.3.sent = bf16[16,32,128]{2,1,0:T(8,128)(2,1)S(1)} custom-call(s32[2,2048]{1,0:T(2,128)S(1)} %copy-done.7, bf16[512,32,128]{2,1,0:T(8,128)(2,1)} %bitcast.values, f32[16,32,128]{2,1,0:T(8,128)S(1)} %baselines.2.rest_0_), custom_call_target="tpu_custom_call" | custom-call | flops 33554432 | bytes 4194304 | tf_op jit(solution)/shard_map/baselines/pallas_call | solution.py:310
  250.8 0.0 copy-start.6
  250.8 0.7 copy-done.6
  251.4 23.8 %exchange.1 = bf16[16,32,128]{2,1,0:T(8,128)(2,1)} custom-call(bf16[16,32,128]{2,1,0:T(8,128)(2,1)} %copy-done.6), custom_call_target="tpu_custom_call" | custom-call | tf_op jit(solution)/shard_map/exchange/pallas_call | solution.py:364
  275.2 0.0 copy-done.8
  275.2 1.2 fusion.12
  276.4 0.7 fusion
Async XLA Ops:
  0.8 3.4 %copy-start = (bf16[32,132608]{1,0:T(8,128)(2,1)S(1)}, bf16[32,132608]{1,0:T(8,128)(2,1)}, u32[]{:S(2)}) copy-start(bf16[32,132608]{1,0:T(8,128)(2,1)} %volts.3) | copy-start | bytes 25460740
  4.2 1.1 copy-start.4
  25.0 2.0 copy-start.3
  26.9 7.6 %copy-start.5 = (bf16[2,256,768]{2,1,0:T(8,128)(2,1)S(1)}, bf16[2,256,768]{2,1,0:T(8,128)(2,1)}, u32[]{:S(2)}) copy-start(bf16[2,256,768]{2,1,0:T(8,128)(2,1)} %constant.63.clone.table_far) | copy-start | bytes 2359300
  26.9 85.2 %all-to-all-start.1 = ((bf16[16,32,32,128]{3,2,1,0:T(8,128)(2,1)}), bf16[16,32,32,128]{3,2,1,0:T(8,128)(2,1)}, u32[]{:S(2)}, u32[]{:S(2)}) async-start(bf16[16,32,32,128]{3,2,1,0:T(8,128)(2,1)} %copy-done.3), calls=%async_computation.1 | async-start | bytes 8388608 | tf_op jit(solution)/shard_map/all_to_all | solution.py:392
  34.5 3.4 %copy-start.1 = (bf16[32,132608]{1,0:T(8,128)(2,1)S(1)}, bf16[32,132608]{1,0:T(8,128)(2,1)}, u32[]{:S(2)}) copy-start(bf16[32,132608]{1,0:T(8,128)(2,1)} %volts.3) | copy-start | bytes 25460740
  57.5 2.0 copy-start.2
  59.5 72.4 %copy-start.7 = (s32[2,2048]{1,0:T(2,128)S(1)}, s32[2,2048]{1,0:T(2,128)}, u32[]{:S(2)}) copy-start(s32[2,2048]{1,0:T(2,128)} %pairs.3) | copy-start | bytes 49156
  112.2 97.4 %all-to-all-start = ((bf16[16,32,32,128]{3,2,1,0:T(8,128)(2,1)}), bf16[16,32,32,128]{3,2,1,0:T(8,128)(2,1)}, u32[]{:S(2)}, u32[]{:S(2)}) async-start(bf16[16,32,32,128]{3,2,1,0:T(8,128)(2,1)} %copy-done.2), calls=%async_computation | async-start | bytes 8388608 | tf_op jit(solution)/shard_map/all_to_all | solution.py:392
  131.9 143.3 %copy-start.8 = (bf16[512,512]{1,0:T(8,128)(2,1)S(1)}, bf16[512,512]{1,0:T(8,128)(2,1)}, u32[]{:S(2)}) copy-start(bf16[512,512]{1,0:T(8,128)(2,1)} %constant.64.clone) | copy-start | bytes 1572868
  250.8 0.7 copy-start.6

commit v2 on v1

--- a/solution.py
+++ b/solution.py
@@ -155,8 +155,8 @@
     angle = 2 * np.pi * (chan[:, None] * chan[None, :] % CHANNEL_COUNT) / CHANNEL_COUNT
     cosine, sine = np.cos(angle) * window, np.sin(angle) * window
     table = np.block([[cosine, sine], [-sine, cosine]]) / np.sqrt(np.sum(window * window))
-    channel = owned_channels(width)[:, :, None, :]
-    order = channel + CHANNEL_COUNT * np.arange(2)[None, None, :, None]
+    channel = owned_channels(width)[:, None, :, :]
+    order = channel + CHANNEL_COUNT * np.arange(2)[None, :, None, None]
     return table[:, order.reshape(-1)].astype(np.float32).astype(ml_dtypes.bfloat16)
 
 
@@ -208,10 +208,11 @@
                     filt[2 + block, rows, :] = sides[0][u] - sides[1][u]
 
     table_copy.wait()
-    rows_each = out.shape[2] // 2
+    width, each = out.shape[0], out.shape[2] // 4
 
     @pl.loop(0, inputs, unroll=2)
     def _(a):
+        results = []
         for parity in range(2):
             x = jnp.concatenate(
                 [filt[2 * parity + b, pl.ds(a, NT, stride=inputs), :] for b in range(2)], axis=1
@@ -224,9 +225,9 @@
                 (((1,), (1,)), ((), ())),
                 preferred_element_type=jnp.float32,
             )
-            out[:, a, parity * rows_each : (parity + 1) * rows_each, :] = result.astype(
-                jnp.bfloat16
-            ).reshape(out.shape[0], rows_each, NT)
+            results.append(result.reshape(width, 2, each, NT))
+        pieces = [results[parity][:, r] for r in range(2) for parity in range(2)]
+        out[:, a] = jnp.concatenate(pieces, axis=1).astype(jnp.bfloat16)
 
 
 def make_spectra(batch, voltages, flags, proto, table, width):
@@ -255,49 +256,35 @@
     )(voltages, flags, proto, table)
 
 
-def fold(parts, shift, lane):
-    first = lane & shift == 0
-    return [
-        jnp.where(first, u, v) + pltpu.roll(jnp.where(first, v, u), shift, 1)
-        for u, v in zip(parts[::2], parts[1::2])
-    ]
-
-
 def baseline_kernel(last, pairs, values, *rest):
-    before, out, partial = rest if last else (None, *rest)
+    before, out = rest if last else (None, rest[0])
     rows = values.shape[1]
-    each = rows // 4
+    each = rows // 2
     lane = lax.broadcasted_iota(jnp.int32, (rows, LANES), 1)
+    ones = jnp.ones((2 * LANES, LANES), jnp.bfloat16)
 
     def products(k):
-        a = values[pairs[0, k]].astype(jnp.float32)
-        b = values[pairs[1, k]].astype(jnp.float32)
-        terms = []
-        for start in (0, 2 * each):
-            a_re, a_im = a[start : start + each], a[start + each : start + 2 * each]
-            b_re, b_im = b[start : start + each], b[start + each : start + 2 * each]
-            terms.append(a_re * b_re + a_im * b_im)
-            terms.append(a_im * b_re - a_re * b_im)
-        return jnp.concatenate(terms, axis=0)
+        a, b = values[pairs[0, k]], values[pairs[1, k]]
+        a_re, a_im, b_re, b_im = a[:each], a[each:], b[:each], b[each:]
+        left = jnp.concatenate([a_re * b_re, a_im * b_re], axis=0)
+        right = jnp.concatenate([a_im * b_im, a_re * -b_im], axis=0)
+        return jnp.concatenate([left, right], axis=1)
 
     @pl.loop(0, out.shape[0])
     def _(block):
-        @pl.loop(0, LANES // TOGETHER, unroll=2)
-        def _(group):
-            start = block * LANES + group * TOGETHER
-            parts = [products(start + at) for at in range(TOGETHER)]
-            shift = 1
-            while len(parts) > 1:
-                parts = fold(parts, shift, lane)
-                shift *= 2
-            partial[group] = parts[0]
-
-        parts = [partial[group] for group in range(LANES // TOGETHER)]
-        shift = TOGETHER
-        while len(parts) > 1:
-            parts = fold(parts, shift, lane)
-            shift *= 2
-        total = parts[0]
+        def some(group, total):
+            first = group * TOGETHER
+            terms = [products(block * LANES + first + at) for at in range(TOGETHER)]
+            sums = jnp.dot(
+                jnp.concatenate(terms, axis=0), ones, preferred_element_type=jnp.float32
+            )
+            for at in range(TOGETHER):
+                total = jnp.where(lane == first + at, sums[at * rows : (at + 1) * rows], total)
+            return total
+
+        total = lax.fori_loop(
+            0, LANES // TOGETHER, some, jnp.zeros((rows, LANES), jnp.float32), unroll=2
+        )
         if last:
             total = (total + before[block]) * (1.0 / math.sqrt(2 * NT))
         out[block] = total.astype(out.dtype)
@@ -314,7 +301,6 @@
         ),
         in_specs=[pl.BlockSpec(memory_space=pltpu.SMEM), vmem] + [vmem] * last,
         out_specs=vmem,
-        scratch_shapes=[pltpu.VMEM((LANES // TOGETHER, rows, LANES), jnp.float32)],
         compiler_params=pltpu.CompilerParams(vmem_limit_bytes=32 * 2**20),
         cost_estimate=pl.CostEstimate(
             flops=4 * count * rows * NT,

time: 278 us -> 267 us (0.960)
  Pallas kernels: 145 us -> 125 us
  waiting for transfers between devices: 89.1 us -> 99.5 us
    pallas_call x2, Pallas kernels: 82.4 us -> 61.7 us  [correlate_baselines(): pl.pallas_call(functools.partial(baseline_kernel, last), out_shape=jax.Sh...]
    all_to_all x2, waiting for transfers between devices: 89.1 us -> 99.5 us  [per_device(): lax.all_to_all(sent, 'wide', split_axis=0, concat_axis=0, tiled=True)]
  transfers between devices with their start and end apart: 2 -> 2, of which waited for: 2 -> 2; matrix products, arithmetic and copies ran while one was open for 0% -> 0% of each run, Pallas kernels for 22% -> 19%
where the time goes in v2:
time: 267 us
  Pallas kernels  125 us (47%)
  waiting for transfers between devices  99.5 us (37%)
  starting transfers between devices  27.3 us (10%)
  local copies, waits for them, and re-layouts  12.6 us (5%)
    all_to_all x2, waiting for transfers between devices, per_device(): lax.all_to_all(sent, 'wide', split_axis=0, concat_axis=0, tiled=True)  99.5 us
    pallas_call x2, Pallas kernels, correlate_baselines(): pl.pallas_call(functools.partial(baseline_kernel, last), out_shape=jax.Sh...  61.7 us
    pallas_call x2, Pallas kernels, make_spectra(): pl.pallas_call(functools.partial(spectra_kernel, batch), out_shape=jax.Sh...  39.2 us
    all_to_all x2, starting transfers between devices, per_device(): lax.all_to_all(sent, 'wide', split_axis=0, concat_axis=0, tiled=True)  27.3 us
    pallas_call x1, Pallas kernels, exchange(): pl.pallas_call(functools.partial(exchange_kernel, width), out_shape=jax.S...  23.8 us
    unnamed x18, local copies, waits for them, and re-layouts  12.5 us
  transfers between devices with their start and end apart: 2, of which 2 were waited for; matrix products, arithmetic and copies ran while one was open for 0% of the time, Pallas kernels for 19%

profile of v2, /device:TPU:0, one launch (start us, length us, event | category | flops | bytes accessed | tf_op | source)
XLA Modules:
  0.0 266.8 jit_solution(17682190486541879282)
XLA Ops:
  0.0 0.1 fusion.6.proto
  0.1 0.7 convert_element_type.8
  0.8 0.1 broadcast_in_dim.11.flags
  0.8 0.0 copy-start
  0.8 3.4 %copy-done = bf16[32,132608]{1,0:T(8,128)(2,1)S(1)} copy-done((bf16[32,132608]{1,0:T(8,128)(2,1)S(1)}, bf16[32,132608]{1,0:T(8,128)(2,1)}, u32[]{:S(2)}) %copy-start) | copy-done | bytes 8486936
  4.2 0.0 copy-start.4
  4.2 1.1 copy-done.4
  5.4 19.6 %spectra.3 = bf16[16,32,32,128]{3,2,1,0:T(8,128)(2,1)S(1)} custom-call(bf16[32,132608]{1,0:T(8,128)(2,1)S(1)} %copy-done, f32[32,128]{1,0:T(8,128)S(1)} %broadcast_in_dim.11.flags, f32[4,512]{1,0:T(4,128)S(1)} %fusion.6.proto, bf16[2,256,768]{2,1,0:T(8,128)(2,1)S(1)} %copy-done.4), custom_call_target="tpu_custom_call" | custom-call | flops 3221225472 | bytes 8388608 | tf_op jit(solution)/shard_map/spectra/pallas_call | solution.py:238
  25.0 0.0 copy-start.3
  25.0 1.9 copy-done.3
  26.9 0.0 copy-start.5
  26.9 7.6 %all-to-all-start.1 = ((bf16[16,32,32,128]{3,2,1,0:T(8,128)(2,1)}), bf16[16,32,32,128]{3,2,1,0:T(8,128)(2,1)}, u32[]{:S(2)}, u32[]{:S(2)}) async-start(bf16[16,32,32,128]{3,2,1,0:T(8,128)(2,1)} %copy-done.3), calls=%async_computation.1 | async-start | bytes 8388608 | tf_op jit(solution)/shard_map/all_to_all | solution.py:378
  34.5 0.0 copy-done.5
  34.5 0.0 copy-start.1
  34.5 3.4 %copy-done.1 = bf16[32,132608]{1,0:T(8,128)(2,1)S(1)} copy-done((bf16[32,132608]{1,0:T(8,128)(2,1)S(1)}, bf16[32,132608]{1,0:T(8,128)(2,1)}, u32[]{:S(2)}) %copy-start.1) | copy-done | bytes 8486936
  37.9 19.6 %spectra.2 = bf16[16,32,32,128]{3,2,1,0:T(8,128)(2,1)S(1)} custom-call(bf16[32,132608]{1,0:T(8,128)(2,1)S(1)} %copy-done.1, f32[32,128]{1,0:T(8,128)S(1)} %broadcast_in_dim.11.flags, f32[4,512]{1,0:T(4,128)S(1)} %fusion.6.proto, bf16[2,256,768]{2,1,0:T(8,128)(2,1)S(1)} %copy-done.5), custom_call_target="tpu_custom_call" | custom-call | flops 3221225472 | bytes 8388608 | tf_op jit(solution)/shard_map/spectra/pallas_call | solution.py:238
  57.6 0.0 copy-start.2
  57.6 2.0 copy-done.2
  59.5 0.0 copy-start.7
  59.5 52.7 %all-to-all-done.1 = bf16[16,32,32,128]{3,2,1,0:T(8,128)(2,1)} async-done(((bf16[16,32,32,128]{3,2,1,0:T(8,128)(2,1)}), bf16[16,32,32,128]{3,2,1,0:T(8,128)(2,1)}, u32[]{:S(2)}, u32[]{:S(2)}) %all-to-all-start.1) | async-done | bytes 4194336 | tf_op jit(solution)/shard_map/all_to_all | solution.py:378
  112.2 19.7 %all-to-all-start = ((bf16[16,32,32,128]{3,2,1,0:T(8,128)(2,1)}), bf16[16,32,32,128]{3,2,1,0:T(8,128)(2,1)}, u32[]{:S(2)}, u32[]{:S(2)}) async-start(bf16[16,32,32,128]{3,2,1,0:T(8,128)(2,1)} %copy-done.2), calls=%async_computation | async-start | bytes 8388608 | tf_op jit(solution)/shard_map/all_to_all | solution.py:378
  131.9 0.0 copy-done.7
  131.9 0.0 copy-start.8
  131.9 30.9 %baselines.2.rest_0_ = f32[16,32,128]{2,1,0:T(8,128)S(1)} custom-call(s32[2,2048]{1,0:T(2,128)S(1)} %copy-done.7, bf16[512,32,128]{2,1,0:T(8,128)(2,1)} %bitcast.1.values), custom_call_target="tpu_custom_call" | custom-call | flops 33554432 | bytes 4194304 | tf_op jit(solution)/shard_map/baselines/pallas_call | solution.py:297
  162.8 46.8 %all-to-all-done = bf16[16,32,32,128]{3,2,1,0:T(8,128)(2,1)} async-done(((bf16[16,32,32,128]{3,2,1,0:T(8,128)(2,1)}), bf16[16,32,32,128]{3,2,1,0:T(8,128)(2,1)}, u32[]{:S(2)}, u32[]{:S(2)}) %all-to-all-start) | async-done | bytes 4194336 | tf_op jit(solution)/shard_map/all_to_all | solution.py:378
  209.6 30.9 %baselines.3.sent = bf16[16,32,128]{2,1,0:T(8,128)(2,1)S(1)} custom-call(s32[2,2048]{1,0:T(2,128)S(1)} %copy-done.7, bf16[512,32,128]{2,1,0:T(8,128)(2,1)} %bitcast.values, f32[16,32,128]{2,1,0:T(8,128)S(1)} %baselines.2.rest_0_), custom_call_target="tpu_custom_call" | custom-call | flops 33554432 | bytes 4194304 | tf_op jit(solution)/shard_map/baselines/pallas_call | solution.py:297
  240.4 0.0 copy-start.6
  240.4 0.6 copy-done.6
  241.1 23.8 %exchange.1 = bf16[16,32,128]{2,1,0:T(8,128)(2,1)} custom-call(bf16[16,32,128]{2,1,0:T(8,128)(2,1)} %copy-done.6), custom_call_target="tpu_custom_call" | custom-call | tf_op jit(solution)/shard_map/exchange/pallas_call | solution.py:350
  264.9 0.0 copy-done.8
  264.9 1.2 fusion.12
  266.1 0.7 fusion
Async XLA Ops:
  0.8 3.4 %copy-start = (bf16[32,132608]{1,0:T(8,128)(2,1)S(1)}, bf16[32,132608]{1,0:T(8,128)(2,1)}, u32[]{:S(2)}) copy-start(bf16[32,132608]{1,0:T(8,128)(2,1)} %volts.3) | copy-start | bytes 25460740
  4.2 1.1 copy-start.4
  25.0 2.0 copy-start.3
  26.9 7.6 %copy-start.5 = (bf16[2,256,768]{2,1,0:T(8,128)(2,1)S(1)}, bf16[2,256,768]{2,1,0:T(8,128)(2,1)}, u32[]{:S(2)}) copy-start(bf16[2,256,768]{2,1,0:T(8,128)(2,1)} %constant.63.clone.table_far) | copy-start | bytes 2359300
  26.9 85.3 %all-to-all-start.1 = ((bf16[16,32,32,128]{3,2,1,0:T(8,128)(2,1)}), bf16[16,32,32,128]{3,2,1,0:T(8,128)(2,1)}, u32[]{:S(2)}, u32[]{:S(2)}) async-start(bf16[16,32,32,128]{3,2,1,0:T(8,128)(2,1)} %copy-done.3), calls=%async_computation.1 | async-start | bytes 8388608 | tf_op jit(solution)/shard_map/all_to_all | solution.py:378
  34.5 3.4 %copy-start.1 = (bf16[32,132608]{1,0:T(8,128)(2,1)S(1)}, bf16[32,132608]{1,0:T(8,128)(2,1)}, u32[]{:S(2)}) copy-start(bf16[32,132608]{1,0:T(8,128)(2,1)} %volts.3) | copy-start | bytes 25460740
  57.6 2.0 copy-start.2
  59.5 72.4 %copy-start.7 = (s32[2,2048]{1,0:T(2,128)S(1)}, s32[2,2048]{1,0:T(2,128)}, u32[]{:S(2)}) copy-start(s32[2,2048]{1,0:T(2,128)} %pairs.3) | copy-start | bytes 49156
  112.2 97.4 %all-to-all-start = ((bf16[16,32,32,128]{3,2,1,0:T(8,128)(2,1)}), bf16[16,32,32,128]{3,2,1,0:T(8,128)(2,1)}, u32[]{:S(2)}, u32[]{:S(2)}) async-start(bf16[16,32,32,128]{3,2,1,0:T(8,128)(2,1)} %copy-done.2), calls=%async_computation | async-start | bytes 8388608 | tf_op jit(solution)/shard_map/all_to_all | solution.py:378
  131.9 133.0 %copy-start.8 = (bf16[512,512]{1,0:T(8,128)(2,1)S(1)}, bf16[512,512]{1,0:T(8,128)(2,1)}, u32[]{:S(2)}) copy-start(bf16[512,512]{1,0:T(8,128)(2,1)} %constant.64.clone) | copy-start | bytes 1572868
  240.4 0.7 copy-start.6

commit v3 on v2

--- a/solution.py
+++ b/solution.py
@@ -126,7 +126,7 @@
 HALF = NFFT // 2
 PIECES = 4
 STEP = 4
-TOGETHER = 8
+TOGETHER = 16
 
 
 def owned_channels(width):

time: 267 us -> 259 us (0.970)
  Pallas kernels: 125 us -> 108 us
  waiting for transfers between devices: 99.5 us -> 108 us
    pallas_call x2, Pallas kernels: 61.7 us -> 45.4 us  [correlate_baselines(): pl.pallas_call(functools.partial(baseline_kernel, last), out_shape=jax.Sh...]
    all_to_all x2, waiting for transfers between devices: 99.5 us -> 108 us  [per_device(): lax.all_to_all(sent, 'wide', split_axis=0, concat_axis=0, tiled=True)]
  transfers between devices with their start and end apart: 2 -> 2, of which waited for: 2 -> 2; matrix products, arithmetic and copies ran while one was open for 0% -> 0% of each run, Pallas kernels for 19% -> 16%
where the time goes in v3:
time: 259 us
  Pallas kernels  108 us (42%)
  waiting for transfers between devices  108 us (42%)
  starting transfers between devices  27.3 us (11%)
  local copies, waits for them, and re-layouts  12.6 us (5%)
    all_to_all x2, waiting for transfers between devices, per_device(): lax.all_to_all(sent, 'wide', split_axis=0, concat_axis=0, tiled=True)  108 us
    pallas_call x2, Pallas kernels, correlate_baselines(): pl.pallas_call(functools.partial(baseline_kernel, last), out_shape=jax.Sh...  45.4 us
    pallas_call x2, Pallas kernels, make_spectra(): pl.pallas_call(functools.partial(spectra_kernel, batch), out_shape=jax.Sh...  39.2 us
    all_to_all x2, starting transfers between devices, per_device(): lax.all_to_all(sent, 'wide', split_axis=0, concat_axis=0, tiled=True)  27.3 us
    pallas_call x1, Pallas kernels, exchange(): pl.pallas_call(functools.partial(exchange_kernel, width), out_shape=jax.S...  23.8 us
    unnamed x18, local copies, waits for them, and re-layouts  12.5 us
  transfers between devices with their start and end apart: 2, of which 2 were waited for; matrix products, arithmetic and copies ran while one was open for 0% of the time, Pallas kernels for 16%

profile of v3, /device:TPU:0, one launch (start us, length us, event | category | flops | bytes accessed | tf_op | source)
XLA Modules:
  0.0 258.7 jit_solution(9245726465281952329)
XLA Ops:
  0.0 0.1 fusion.6.proto
  0.1 0.7 convert_element_type.8
  0.8 0.1 broadcast_in_dim.11.flags
  0.8 0.0 copy-start
  0.8 3.4 %copy-done = bf16[32,132608]{1,0:T(8,128)(2,1)S(1)} copy-done((bf16[32,132608]{1,0:T(8,128)(2,1)S(1)}, bf16[32,132608]{1,0:T(8,128)(2,1)}, u32[]{:S(2)}) %copy-start) | copy-done | bytes 8486936
  4.2 0.0 copy-start.4
  4.2 1.1 copy-done.4
  5.4 19.6 %spectra.3 = bf16[16,32,32,128]{3,2,1,0:T(8,128)(2,1)S(1)} custom-call(bf16[32,132608]{1,0:T(8,128)(2,1)S(1)} %copy-done, f32[32,128]{1,0:T(8,128)S(1)} %broadcast_in_dim.11.flags, f32[4,512]{1,0:T(4,128)S(1)} %fusion.6.proto, bf16[2,256,768]{2,1,0:T(8,128)(2,1)S(1)} %copy-done.4), custom_call_target="tpu_custom_call" | custom-call | flops 3221225472 | bytes 8388608 | tf_op jit(solution)/shard_map/spectra/pallas_call | solution.py:238
  25.0 0.0 copy-start.3
  25.0 1.9 copy-done.3
  26.9 0.0 copy-start.5
  26.9 7.6 %all-to-all-start.1 = ((bf16[16,32,32,128]{3,2,1,0:T(8,128)(2,1)}), bf16[16,32,32,128]{3,2,1,0:T(8,128)(2,1)}, u32[]{:S(2)}, u32[]{:S(2)}) async-start(bf16[16,32,32,128]{3,2,1,0:T(8,128)(2,1)} %copy-done.3), calls=%async_computation.1 | async-start | bytes 8388608 | tf_op jit(solution)/shard_map/all_to_all | solution.py:378
  34.5 0.0 copy-done.5
  34.5 0.0 copy-start.1
  34.5 3.4 %copy-done.1 = bf16[32,132608]{1,0:T(8,128)(2,1)S(1)} copy-done((bf16[32,132608]{1,0:T(8,128)(2,1)S(1)}, bf16[32,132608]{1,0:T(8,128)(2,1)}, u32[]{:S(2)}) %copy-start.1) | copy-done | bytes 8486936
  37.9 19.6 %spectra.2 = bf16[16,32,32,128]{3,2,1,0:T(8,128)(2,1)S(1)} custom-call(bf16[32,132608]{1,0:T(8,128)(2,1)S(1)} %copy-done.1, f32[32,128]{1,0:T(8,128)S(1)} %broadcast_in_dim.11.flags, f32[4,512]{1,0:T(4,128)S(1)} %fusion.6.proto, bf16[2,256,768]{2,1,0:T(8,128)(2,1)S(1)} %copy-done.5), custom_call_target="tpu_custom_call" | custom-call | flops 3221225472 | bytes 8388608 | tf_op jit(solution)/shard_map/spectra/pallas_call | solution.py:238
  57.6 0.0 copy-start.2
  57.6 2.0 copy-done.2
  59.5 0.0 copy-start.7
  59.5 52.7 %all-to-all-done.1 = bf16[16,32,32,128]{3,2,1,0:T(8,128)(2,1)} async-done(((bf16[16,32,32,128]{3,2,1,0:T(8,128)(2,1)}), bf16[16,32,32,128]{3,2,1,0:T(8,128)(2,1)}, u32[]{:S(2)}, u32[]{:S(2)}) %all-to-all-start.1) | async-done | bytes 4194336 | tf_op jit(solution)/shard_map/all_to_all | solution.py:378
  112.2 19.7 %all-to-all-start = ((bf16[16,32,32,128]{3,2,1,0:T(8,128)(2,1)}), bf16[16,32,32,128]{3,2,1,0:T(8,128)(2,1)}, u32[]{:S(2)}, u32[]{:S(2)}) async-start(bf16[16,32,32,128]{3,2,1,0:T(8,128)(2,1)} %copy-done.2), calls=%async_computation | async-start | bytes 8388608 | tf_op jit(solution)/shard_map/all_to_all | solution.py:378
  131.9 0.0 copy-done.7
  131.9 0.0 copy-start.8
  131.9 22.6 %baselines.2.rest_0_ = f32[16,32,128]{2,1,0:T(8,128)S(1)} custom-call(s32[2,2048]{1,0:T(2,128)S(1)} %copy-done.7, bf16[512,32,128]{2,1,0:T(8,128)(2,1)} %bitcast.1.values), custom_call_target="tpu_custom_call" | custom-call | flops 33554432 | bytes 4194304 | tf_op jit(solution)/shard_map/baselines/pallas_call | solution.py:297
  154.6 55.0 %all-to-all-done = bf16[16,32,32,128]{3,2,1,0:T(8,128)(2,1)} async-done(((bf16[16,32,32,128]{3,2,1,0:T(8,128)(2,1)}), bf16[16,32,32,128]{3,2,1,0:T(8,128)(2,1)}, u32[]{:S(2)}, u32[]{:S(2)}) %all-to-all-start) | async-done | bytes 4194336 | tf_op jit(solution)/shard_map/all_to_all | solution.py:378
  209.6 22.8 %baselines.3.sent = bf16[16,32,128]{2,1,0:T(8,128)(2,1)S(1)} custom-call(s32[2,2048]{1,0:T(2,128)S(1)} %copy-done.7, bf16[512,32,128]{2,1,0:T(8,128)(2,1)} %bitcast.values, f32[16,32,128]{2,1,0:T(8,128)S(1)} %baselines.2.rest_0_), custom_call_target="tpu_custom_call" | custom-call | flops 33554432 | bytes 4194304 | tf_op jit(solution)/shard_map/baselines/pallas_call | solution.py:297
  232.4 0.0 copy-start.6
  232.4 0.6 copy-done.6
  233.0 23.8 %exchange.1 = bf16[16,32,128]{2,1,0:T(8,128)(2,1)} custom-call(bf16[16,32,128]{2,1,0:T(8,128)(2,1)} %copy-done.6), custom_call_target="tpu_custom_call" | custom-call | tf_op jit(solution)/shard_map/exchange/pallas_call | solution.py:350
  256.8 0.0 copy-done.8
  256.8 1.2 fusion.12
  258.0 0.7 fusion
Async XLA Ops:
  0.8 3.4 %copy-start = (bf16[32,132608]{1,0:T(8,128)(2,1)S(1)}, bf16[32,132608]{1,0:T(8,128)(2,1)}, u32[]{:S(2)}) copy-start(bf16[32,132608]{1,0:T(8,128)(2,1)} %volts.3) | copy-start | bytes 25460740
  4.2 1.1 copy-start.4
  25.0 2.0 copy-start.3
  26.9 7.6 %copy-start.5 = (bf16[2,256,768]{2,1,0:T(8,128)(2,1)S(1)}, bf16[2,256,768]{2,1,0:T(8,128)(2,1)}, u32[]{:S(2)}) copy-start(bf16[2,256,768]{2,1,0:T(8,128)(2,1)} %constant.63.clone.table_far) | copy-start | bytes 2359300
  26.9 85.3 %all-to-all-start.1 = ((bf16[16,32,32,128]{3,2,1,0:T(8,128)(2,1)}), bf16[16,32,32,128]{3,2,1,0:T(8,128)(2,1)}, u32[]{:S(2)}, u32[]{:S(2)}) async-start(bf16[16,32,32,128]{3,2,1,0:T(8,128)(2,1)} %copy-done.3), calls=%async_computation.1 | async-start | bytes 8388608 | tf_op jit(solution)/shard_map/all_to_all | solution.py:378
  34.5 3.4 %copy-start.1 = (bf16[32,132608]{1,0:T(8,128)(2,1)S(1)}, bf16[32,132608]{1,0:T(8,128)(2,1)}, u32[]{:S(2)}) copy-start(bf16[32,132608]{1,0:T(8,128)(2,1)} %volts.3) | copy-start | bytes 25460740
  57.6 2.0 copy-start.2
  59.5 72.4 %copy-start.7 = (s32[2,2048]{1,0:T(2,128)S(1)}, s32[2,2048]{1,0:T(2,128)}, u32[]{:S(2)}) copy-start(s32[2,2048]{1,0:T(2,128)} %pairs.3) | copy-start | bytes 49156
  112.2 97.4 %all-to-all-start = ((bf16[16,32,32,128]{3,2,1,0:T(8,128)(2,1)}), bf16[16,32,32,128]{3,2,1,0:T(8,128)(2,1)}, u32[]{:S(2)}, u32[]{:S(2)}) async-start(bf16[16,32,32,128]{3,2,1,0:T(8,128)(2,1)} %copy-done.2), calls=%async_computation | async-start | bytes 8388608 | tf_op jit(solution)/shard_map/all_to_all | solution.py:378
  131.9 124.9 %copy-start.8 = (bf16[512,512]{1,0:T(8,128)(2,1)S(1)}, bf16[512,512]{1,0:T(8,128)(2,1)}, u32[]{:S(2)}) copy-start(bf16[512,512]{1,0:T(8,128)(2,1)} %constant.64.clone) | copy-start | bytes 1572868
  232.4 0.7 copy-start.6
